TPU v7x, 256 devices: a whole 4x4x8 slice. The times are simulated.
256 devices in a mesh: gz: 16 (over z, core), gy: 8 (over y, x_hi), orb: 2 (over x_lo).
Axes of the slice: x: 4 (x_hi: 2, x_lo: 2; x = x_hi * 2 + x_lo), y: 4, z: 8, core: 2. Of those that a mesh axis runs over, the one named last changes fastest.
Arguments:
- orbitals: bfloat16 [4096, 24, 576], P(('gz', 'gy', 'orb')), may hold values from -6 to 6
- occupation: float32 [4096], P(('gz', 'gy', 'orb')), may hold values from 0.5 to 2
- corners: int32 [4096, 3], P(('gz', 'gy', 'orb')), may hold values from 0 to 383, as said below
- kernel_widths: float32 [8], replicated, may hold values from 0.7 to 2.5
- w_in: float32 [8, 64], replicated, may hold values from -2 to 2
- b_in: float32 [64], replicated, may hold values from -3 to 3
- w_mid: float32 [64, 64], replicated, may hold values from -0.75 to 0.75
- b_mid: float32 [64], replicated, may hold values from -3 to 3
- w_out: float32 [64], replicated, may hold values from -0.75 to 0.75
- b_out: float32 [1], replicated, may hold values from -3 to 3
Outputs:
- potential: bfloat16 [384, 192, 128], P('gz', 'gy')
- applied: bfloat16 [4096, 24, 576], P(('gz', 'gy', 'orb'))
Inputs may be any that keep to these rules, and one draw needn't show every extreme that they name: Orbital i is held by device i // 16 of the axes gz, gy, orb taken together. Its row corners[i,1] lies in the 24 rows of that device's gy index. Among the 16 orbitals of one device, at most 2 have their plane corners[i,0] in the same slab of 24 planes, and on every device some slab holds exactly 2 of them. Columns lie in 0 to 127, rows in 0 to 191, planes in 0 to 383; the first and the last plane are taken in every draw.
All inputs are finite; a program needn't handle non-finite values.
Results may differ from a plain program's by a relative error of at most 0.0055.
Values may be sent and summed in bfloat16 or wider, within the bound.
No kernel may reach another device: no remote copies, remote signals or barrier semaphores. Data moves between devices by JAX's collectives and lax.ppermute only.
A program may use at most 64 MiB of HBM per device.

v0:
```python
import jax
import jax.numpy as jnp
from jax import lax
from jax.sharding import PartitionSpec as P

BOX = 24
CHAN = 8
RAD = 6
CZ = 24
CY = 24
NX = 128
CAP = 2
CELL_BLOCK = 12288
exact_mode = lax.Precision.HIGHEST


def shifted(x, axis, by):
    count = lax.axis_size(axis)
    return lax.ppermute(x, axis, [(i, (i + by) % count) for i in range(count)])


def extended_2(cells, sides, width):
    for axis, dim in sides:
        count = lax.axis_size(axis)
        head = lax.slice_in_dim(cells, 0, width, axis=dim)
        tail = lax.slice_in_dim(cells, cells.shape[dim] - width, cells.shape[dim], axis=dim)
        cells = jnp.concatenate(
            [
                lax.ppermute(tail, axis, [(i, (i + 1) % count) for i in range(count)]),
                cells,
                lax.ppermute(head, axis, [((i + 1) % count, i) for i in range(count)]),
            ],
            axis=dim,
        )
    return cells


def for_sending(x):
    return jax.tree.map(lambda a: a.astype(jnp.bfloat16) if a.dtype == jnp.float32 else a, x)


def kernel_taps(kernel_widths):
    offsets = jnp.arange(-RAD, RAD + 1).astype(jnp.float32)
    raw = jnp.exp(-offsets[None, :] ** 2 / (2.0 * kernel_widths[:, None] ** 2))
    return raw / jnp.sum(raw, axis=1, keepdims=True)


def tap_table(taps, distance):
    table = jnp.zeros((taps.shape[0],) + distance.shape, jnp.float32)
    for step in range(2 * RAD + 1):
        table = table + taps[:, step][:, None, None] * (distance == step).astype(jnp.float32)[None]
    return table


def smooth_all(padded, taps, planes, rows):
    columns = padded.shape[2]
    source = jnp.arange(columns, dtype=jnp.int32)
    circular = (source[:, None] - source[None, :] + RAD) % columns
    across_table = tap_table(taps, circular)
    across = jnp.einsum("prs,kst->kprt", padded, across_table, precision=exact_mode)
    row_out = jnp.arange(rows, dtype=jnp.int32)
    row_in = jnp.arange(rows + 2 * RAD, dtype=jnp.int32)
    row_table = tap_table(taps, row_in[None, :] - row_out[:, None])
    lines = jnp.einsum("kqr,kprt->kpqt", row_table, across, precision=exact_mode)
    plane_out = jnp.arange(planes, dtype=jnp.int32)
    plane_in = jnp.arange(planes + 2 * RAD, dtype=jnp.int32)
    plane_table = tap_table(taps, plane_in[None, :] - plane_out[:, None])
    return jnp.einsum("kop,kpqt->koqt", plane_table, lines, precision=exact_mode)


def network(features, w_in, b_in, w_mid, b_mid, w_out, b_out):
    count = features.shape[1]
    blocks = features.reshape(CHAN, count // CELL_BLOCK, CELL_BLOCK).transpose(1, 0, 2)

    def layer_stack(block):
        hidden = jax.nn.silu(jnp.dot(w_in.T, block, precision=exact_mode) + b_in[:, None])
        hidden = jax.nn.silu(jnp.dot(w_mid.T, hidden, precision=exact_mode) + b_mid[:, None])
        return jnp.dot(w_out, hidden, precision=exact_mode) + b_out[0]

    return lax.map(layer_stack, blocks).reshape(count)


def local(orbitals, occupation, corners, kernel_widths, w_in, b_in, w_mid, b_mid, w_out, b_out):
    slab_count = lax.axis_size("gz")
    slot_count = slab_count * CAP
    held = orbitals.shape[0]
    orbital_vals = orbitals.astype(jnp.float32)
    box_density = (occupation[:, None, None] * orbital_vals * orbital_vals).astype(jnp.bfloat16)
    box_density = box_density.reshape(held, BOX**3)
    target = corners[:, 0] // CZ
    orbital_ids = jnp.arange(held, dtype=jnp.int32)
    earlier = (target[:, None] == target[None, :]) & (orbital_ids[None, :] < orbital_ids[:, None])
    slot_rank = jnp.sum(earlier.astype(jnp.int32), axis=1)
    slot_of = target * CAP + slot_rank
    placer = (jnp.arange(slot_count, dtype=jnp.int32)[:, None] == slot_of[None, :]).astype(
        jnp.bfloat16
    )
    local_offsets = jnp.stack(
        [corners[:, 0] % CZ, corners[:, 1] % CY, corners[:, 2]], axis=1
    ).astype(jnp.bfloat16)
    sent = jnp.dot(placer, box_density, preferred_element_type=jnp.float32).astype(jnp.bfloat16)
    sent_offsets = jnp.dot(placer, local_offsets, preferred_element_type=jnp.float32).astype(
        jnp.bfloat16
    )
    received, received_offsets = (
        lax.all_to_all(
            sent.reshape(slab_count, CAP, BOX**3), "gz", split_axis=0, concat_axis=0, tiled=True
        ),
        lax.all_to_all(
            sent_offsets.reshape(slab_count, CAP, 3), "gz", split_axis=0, concat_axis=0, tiled=True
        ),
    )
    offsets = received_offsets.astype(jnp.float32).astype(jnp.int32)

    def deposit(source, grid):
        for column in range(CAP):
            piece = received[source, column].astype(jnp.float32).reshape(BOX, BOX, BOX)
            start = (
                offsets[source, column, 0],
                offsets[source, column, 1],
                offsets[source, column, 2],
            )
            region = lax.dynamic_slice(grid, start, (BOX, BOX, BOX))
            grid = lax.dynamic_update_slice(grid, region + piece, start)
        return grid

    extended = lax.fori_loop(
        0, slab_count, deposit, jnp.zeros((CZ + BOX, CY + BOX, NX + BOX), jnp.float32)
    )
    extended = extended[:, :, :NX].at[:, :, :BOX].add(extended[:, :, NX:])
    from_below = shifted(extended[CZ:].astype(jnp.bfloat16), "gz", 1).astype(jnp.float32)
    core = extended[:CZ].at[:BOX].add(from_below)
    from_left = shifted(core[:, CY:].astype(jnp.bfloat16), "gy", 1).astype(jnp.float32)
    tile = core[:, :CY].at[:, :BOX].add(from_left)
    density = lax.psum(tile.astype(jnp.bfloat16), "orb").astype(jnp.float32)
    padded = extended_2(density.astype(jnp.bfloat16), (("gz", 0), ("gy", 1)), RAD).astype(
        density.dtype
    )
    taps = kernel_taps(kernel_widths)
    features = jnp.log1p(smooth_all(padded, taps, CZ, CY))
    values = network(features.reshape(CHAN, CZ * CY * NX), w_in, b_in, w_mid, b_mid, w_out, b_out)
    potential = values.reshape(CZ, CY, NX).astype(jnp.bfloat16)
    next_rows = shifted(potential, "gy", -1)
    wide = jnp.concatenate([potential, next_rows], axis=1)
    next_planes = shifted(wide, "gz", -1)
    reach = jnp.concatenate([wide, next_planes], axis=0)
    reach = jnp.concatenate([reach, reach[:, :, :BOX]], axis=2)

    def cut(offset_row):
        windows = []
        for column in range(CAP):
            start = (offset_row[column, 0], offset_row[column, 1], offset_row[column, 2])
            window = lax.dynamic_slice(reach, start, (BOX, BOX, BOX))
            windows.append(window.reshape(BOX**3))
        return jnp.stack(windows)

    windows = lax.map(cut, offsets)
    returned = jax.tree.map(
        lambda part, own: part.astype(own.dtype),
        lax.all_to_all(for_sending(windows), "gz", split_axis=0, concat_axis=0, tiled=True),
        windows,
    )
    on_boxes = jnp.dot(
        placer.T, returned.reshape(slot_count, BOX**3), preferred_element_type=jnp.float32
    )
    applied = (on_boxes.reshape(held, BOX, BOX * BOX) * orbital_vals).astype(jnp.bfloat16)
    return (potential, applied)


def solution(mesh):
    return jax.shard_map(
        local,
        mesh=mesh,
        in_specs=(
            P(("gz", "gy", "orb"), None, None),
            P(("gz", "gy", "orb")),
            P(("gz", "gy", "orb"), None),
            P(),
            P(),
            P(),
            P(),
            P(),
            P(),
            P(),
        ),
        out_specs=(P("gz", "gy", None), P(("gz", "gy", "orb"), None, None)),
        check_vma=False,
    )
```

profile of v0, /device:TPU:1, one launch (start us, length us, event | category | flops | bytes accessed | tf_op | source)
XLA Modules:
  0.0 1365.4 jit_solution(875957933590389903)
XLA Ops:
  10.4 10.0 all-to-all-start
  23.9 3.5 all-to-all-done
  27.3 4.7 all-to-all-start.1
  37.6 19.2 %all-to-all-done.1 = bf16[16,2,13824]{2,1,0:T(2,128)(2,1)} async-done(((bf16[16,2,13824]{2,1,0:T(2,128)(2,1)}), bf16[16,2,13824]{2,1,0:T(2,128)(2,1)}, u32[]{:S(2)}, u32[]{:S(2)}) %all-to-all-start.1) | async-done | bytes 884768 | tf_op jit(solution)/shard_map/all_to_all | solution.py:106
  57.1 825.2 %while.38 = (s32[]{:T(128)}, f32[48,48,152]{2,1,0:T(8,128)S(1)}, s32[16,2,3]{0,1,2:T(2,128)S(1)}, bf16[16,2,13824]{2,1,0:T(2,128)(2,1)}, s32[]{:T(128)}, /*index=5*/s32[]{:T(128)}, s32[]{:T(128)}, s32[]{:T(128)}) while((s32[]{:T(128)}, f32[48,48,152]{2,1,0:T(8,128)S(1)}, s32[16,2,3]{0,1,2:T(2,128)S(1)}, bf16[16,2,13824]{2,1,0:T(2,128)(2,1)}, ...), condition=%wide.region_3.4_spmd, body=%wide.region_2.3_spmd.sunk | while | flops 55316 | bytes 940409 | solution.py:127
  65.0 16.9 %dynamic_update_slice.27 = f32[48,48,152]{2,1,0:T(8,128)S(1)} dynamic-update-slice(f32[48,48,152]{2,1,0:T(8,128)S(1)} %get-tuple-element.505, f32[24,24,24]{2,1,0:T(8,128)S(1)} %dynamic-slice_add_fusion.4, s32[]{:T(128)S(6)} %select_n.230, s32[]{:T(128)S(6)} %select_n.231, s32[]{:T(128)S(6)} %select_n.232) | dynamic-update-slice | bytes 110596 | tf_op jit(solution)/shard_map/while/body/eval_jaxpr/dynamic_update_slice | solution.py:124
  88.4 16.8 %dynamic_update_slice.28 = f32[48,48,152]{2,1,0:T(8,128)S(1)} dynamic-update-slice(f32[48,48,152]{2,1,0:T(8,128)S(1)} %dynamic_update_slice.27, f32[24,24,24]{2,1,0:T(8,128)S(1)} %dynamic-slice_add_fusion.5, s32[]{:T(128)S(6)} %select_n.233, s32[]{:T(128)S(6)} %select_n.234, s32[]{:T(128)S(6)} %select_n.235) | dynamic-update-slice | bytes 110596 | tf_op jit(solution)/shard_map/while/body/eval_jaxpr/dynamic_update_slice | solution.py:124
  113.0 23.0 %dynamic_update_slice.27 = f32[48,48,152]{2,1,0:T(8,128)S(1)} dynamic-update-slice(f32[48,48,152]{2,1,0:T(8,128)S(1)} %get-tuple-element.505, f32[24,24,24]{2,1,0:T(8,128)S(1)} %dynamic-slice_add_fusion.4, s32[]{:T(128)S(6)} %select_n.230, s32[]{:T(128)S(6)} %select_n.231, s32[]{:T(128)S(6)} %select_n.232) | dynamic-update-slice | bytes 110596 | tf_op jit(solution)/shard_map/while/body/eval_jaxpr/dynamic_update_slice | solution.py:124
  142.6 20.9 %dynamic_update_slice.28 = f32[48,48,152]{2,1,0:T(8,128)S(1)} dynamic-update-slice(f32[48,48,152]{2,1,0:T(8,128)S(1)} %dynamic_update_slice.27, f32[24,24,24]{2,1,0:T(8,128)S(1)} %dynamic-slice_add_fusion.5, s32[]{:T(128)S(6)} %select_n.233, s32[]{:T(128)S(6)} %select_n.234, s32[]{:T(128)S(6)} %select_n.235) | dynamic-update-slice | bytes 110596 | tf_op jit(solution)/shard_map/while/body/eval_jaxpr/dynamic_update_slice | solution.py:124
  171.3 22.8 %dynamic_update_slice.27 = f32[48,48,152]{2,1,0:T(8,128)S(1)} dynamic-update-slice(f32[48,48,152]{2,1,0:T(8,128)S(1)} %get-tuple-element.505, f32[24,24,24]{2,1,0:T(8,128)S(1)} %dynamic-slice_add_fusion.4, s32[]{:T(128)S(6)} %select_n.230, s32[]{:T(128)S(6)} %select_n.231, s32[]{:T(128)S(6)} %select_n.232) | dynamic-update-slice | bytes 110596 | tf_op jit(solution)/shard_map/while/body/eval_jaxpr/dynamic_update_slice | solution.py:124
  200.7 16.8 %dynamic_update_slice.28 = f32[48,48,152]{2,1,0:T(8,128)S(1)} dynamic-update-slice(f32[48,48,152]{2,1,0:T(8,128)S(1)} %dynamic_update_slice.27, f32[24,24,24]{2,1,0:T(8,128)S(1)} %dynamic-slice_add_fusion.5, s32[]{:T(128)S(6)} %select_n.233, s32[]{:T(128)S(6)} %select_n.234, s32[]{:T(128)S(6)} %select_n.235) | dynamic-update-slice | bytes 110596 | tf_op jit(solution)/shard_map/while/body/eval_jaxpr/dynamic_update_slice | solution.py:124
  225.3 20.7 %dynamic_update_slice.27 = f32[48,48,152]{2,1,0:T(8,128)S(1)} dynamic-update-slice(f32[48,48,152]{2,1,0:T(8,128)S(1)} %get-tuple-element.505, f32[24,24,24]{2,1,0:T(8,128)S(1)} %dynamic-slice_add_fusion.4, s32[]{:T(128)S(6)} %select_n.230, s32[]{:T(128)S(6)} %select_n.231, s32[]{:T(128)S(6)} %select_n.232) | dynamic-update-slice | bytes 110596 | tf_op jit(solution)/shard_map/while/body/eval_jaxpr/dynamic_update_slice | solution.py:124
  252.6 16.8 %dynamic_update_slice.28 = f32[48,48,152]{2,1,0:T(8,128)S(1)} dynamic-update-slice(f32[48,48,152]{2,1,0:T(8,128)S(1)} %dynamic_update_slice.27, f32[24,24,24]{2,1,0:T(8,128)S(1)} %dynamic-slice_add_fusion.5, s32[]{:T(128)S(6)} %select_n.233, s32[]{:T(128)S(6)} %select_n.234, s32[]{:T(128)S(6)} %select_n.235) | dynamic-update-slice | bytes 110596 | tf_op jit(solution)/shard_map/while/body/eval_jaxpr/dynamic_update_slice | solution.py:124
  277.2 19.7 %dynamic_update_slice.27 = f32[48,48,152]{2,1,0:T(8,128)S(1)} dynamic-update-slice(f32[48,48,152]{2,1,0:T(8,128)S(1)} %get-tuple-element.505, f32[24,24,24]{2,1,0:T(8,128)S(1)} %dynamic-slice_add_fusion.4, s32[]{:T(128)S(6)} %select_n.230, s32[]{:T(128)S(6)} %select_n.231, s32[]{:T(128)S(6)} %select_n.232) | dynamic-update-slice | bytes 110596 | tf_op jit(solution)/shard_map/while/body/eval_jaxpr/dynamic_update_slice | solution.py:124
  303.5 16.8 %dynamic_update_slice.28 = f32[48,48,152]{2,1,0:T(8,128)S(1)} dynamic-update-slice(f32[48,48,152]{2,1,0:T(8,128)S(1)} %dynamic_update_slice.27, f32[24,24,24]{2,1,0:T(8,128)S(1)} %dynamic-slice_add_fusion.5, s32[]{:T(128)S(6)} %select_n.233, s32[]{:T(128)S(6)} %select_n.234, s32[]{:T(128)S(6)} %select_n.235) | dynamic-update-slice | bytes 110596 | tf_op jit(solution)/shard_map/while/body/eval_jaxpr/dynamic_update_slice | solution.py:124
  328.2 16.8 %dynamic_update_slice.27 = f32[48,48,152]{2,1,0:T(8,128)S(1)} dynamic-update-slice(f32[48,48,152]{2,1,0:T(8,128)S(1)} %get-tuple-element.505, f32[24,24,24]{2,1,0:T(8,128)S(1)} %dynamic-slice_add_fusion.4, s32[]{:T(128)S(6)} %select_n.230, s32[]{:T(128)S(6)} %select_n.231, s32[]{:T(128)S(6)} %select_n.232) | dynamic-update-slice | bytes 110596 | tf_op jit(solution)/shard_map/while/body/eval_jaxpr/dynamic_update_slice | solution.py:124
  351.5 16.8 %dynamic_update_slice.28 = f32[48,48,152]{2,1,0:T(8,128)S(1)} dynamic-update-slice(f32[48,48,152]{2,1,0:T(8,128)S(1)} %dynamic_update_slice.27, f32[24,24,24]{2,1,0:T(8,128)S(1)} %dynamic-slice_add_fusion.5, s32[]{:T(128)S(6)} %select_n.233, s32[]{:T(128)S(6)} %select_n.234, s32[]{:T(128)S(6)} %select_n.235) | dynamic-update-slice | bytes 110596 | tf_op jit(solution)/shard_map/while/body/eval_jaxpr/dynamic_update_slice | solution.py:124
  376.2 22.1 %dynamic_update_slice.27 = f32[48,48,152]{2,1,0:T(8,128)S(1)} dynamic-update-slice(f32[48,48,152]{2,1,0:T(8,128)S(1)} %get-tuple-element.505, f32[24,24,24]{2,1,0:T(8,128)S(1)} %dynamic-slice_add_fusion.4, s32[]{:T(128)S(6)} %select_n.230, s32[]{:T(128)S(6)} %select_n.231, s32[]{:T(128)S(6)} %select_n.232) | dynamic-update-slice | bytes 110596 | tf_op jit(solution)/shard_map/while/body/eval_jaxpr/dynamic_update_slice | solution.py:124
  404.8 16.8 %dynamic_update_slice.28 = f32[48,48,152]{2,1,0:T(8,128)S(1)} dynamic-update-slice(f32[48,48,152]{2,1,0:T(8,128)S(1)} %dynamic_update_slice.27, f32[24,24,24]{2,1,0:T(8,128)S(1)} %dynamic-slice_add_fusion.5, s32[]{:T(128)S(6)} %select_n.233, s32[]{:T(128)S(6)} %select_n.234, s32[]{:T(128)S(6)} %select_n.235) | dynamic-update-slice | bytes 110596 | tf_op jit(solution)/shard_map/while/body/eval_jaxpr/dynamic_update_slice | solution.py:124
  429.4 21.6 %dynamic_update_slice.27 = f32[48,48,152]{2,1,0:T(8,128)S(1)} dynamic-update-slice(f32[48,48,152]{2,1,0:T(8,128)S(1)} %get-tuple-element.505, f32[24,24,24]{2,1,0:T(8,128)S(1)} %dynamic-slice_add_fusion.4, s32[]{:T(128)S(6)} %select_n.230, s32[]{:T(128)S(6)} %select_n.231, s32[]{:T(128)S(6)} %select_n.232) | dynamic-update-slice | bytes 110596 | tf_op jit(solution)/shard_map/while/body/eval_jaxpr/dynamic_update_slice | solution.py:124
  457.6 19.7 %dynamic_update_slice.28 = f32[48,48,152]{2,1,0:T(8,128)S(1)} dynamic-update-slice(f32[48,48,152]{2,1,0:T(8,128)S(1)} %dynamic_update_slice.27, f32[24,24,24]{2,1,0:T(8,128)S(1)} %dynamic-slice_add_fusion.5, s32[]{:T(128)S(6)} %select_n.233, s32[]{:T(128)S(6)} %select_n.234, s32[]{:T(128)S(6)} %select_n.235) | dynamic-update-slice | bytes 110596 | tf_op jit(solution)/shard_map/while/body/eval_jaxpr/dynamic_update_slice | solution.py:124
  485.2 17.9 %dynamic_update_slice.27 = f32[48,48,152]{2,1,0:T(8,128)S(1)} dynamic-update-slice(f32[48,48,152]{2,1,0:T(8,128)S(1)} %get-tuple-element.505, f32[24,24,24]{2,1,0:T(8,128)S(1)} %dynamic-slice_add_fusion.4, s32[]{:T(128)S(6)} %select_n.230, s32[]{:T(128)S(6)} %select_n.231, s32[]{:T(128)S(6)} %select_n.232) | dynamic-update-slice | bytes 110596 | tf_op jit(solution)/shard_map/while/body/eval_jaxpr/dynamic_update_slice | solution.py:124
  509.6 19.5 %dynamic_update_slice.28 = f32[48,48,152]{2,1,0:T(8,128)S(1)} dynamic-update-slice(f32[48,48,152]{2,1,0:T(8,128)S(1)} %dynamic_update_slice.27, f32[24,24,24]{2,1,0:T(8,128)S(1)} %dynamic-slice_add_fusion.5, s32[]{:T(128)S(6)} %select_n.233, s32[]{:T(128)S(6)} %select_n.234, s32[]{:T(128)S(6)} %select_n.235) | dynamic-update-slice | bytes 110596 | tf_op jit(solution)/shard_map/while/body/eval_jaxpr/dynamic_update_slice | solution.py:124
  537.0 18.6 %dynamic_update_slice.27 = f32[48,48,152]{2,1,0:T(8,128)S(1)} dynamic-update-slice(f32[48,48,152]{2,1,0:T(8,128)S(1)} %get-tuple-element.505, f32[24,24,24]{2,1,0:T(8,128)S(1)} %dynamic-slice_add_fusion.4, s32[]{:T(128)S(6)} %select_n.230, s32[]{:T(128)S(6)} %select_n.231, s32[]{:T(128)S(6)} %select_n.232) | dynamic-update-slice | bytes 110596 | tf_op jit(solution)/shard_map/while/body/eval_jaxpr/dynamic_update_slice | solution.py:124
  562.1 16.8 %dynamic_update_slice.28 = f32[48,48,152]{2,1,0:T(8,128)S(1)} dynamic-update-slice(f32[48,48,152]{2,1,0:T(8,128)S(1)} %dynamic_update_slice.27, f32[24,24,24]{2,1,0:T(8,128)S(1)} %dynamic-slice_add_fusion.5, s32[]{:T(128)S(6)} %select_n.233, s32[]{:T(128)S(6)} %select_n.234, s32[]{:T(128)S(6)} %select_n.235) | dynamic-update-slice | bytes 110596 | tf_op jit(solution)/shard_map/while/body/eval_jaxpr/dynamic_update_slice | solution.py:124
  586.8 19.4 %dynamic_update_slice.27 = f32[48,48,152]{2,1,0:T(8,128)S(1)} dynamic-update-slice(f32[48,48,152]{2,1,0:T(8,128)S(1)} %get-tuple-element.505, f32[24,24,24]{2,1,0:T(8,128)S(1)} %dynamic-slice_add_fusion.4, s32[]{:T(128)S(6)} %select_n.230, s32[]{:T(128)S(6)} %select_n.231, s32[]{:T(128)S(6)} %select_n.232) | dynamic-update-slice | bytes 110596 | tf_op jit(solution)/shard_map/while/body/eval_jaxpr/dynamic_update_slice | solution.py:124
  612.8 16.8 %dynamic_update_slice.28 = f32[48,48,152]{2,1,0:T(8,128)S(1)} dynamic-update-slice(f32[48,48,152]{2,1,0:T(8,128)S(1)} %dynamic_update_slice.27, f32[24,24,24]{2,1,0:T(8,128)S(1)} %dynamic-slice_add_fusion.5, s32[]{:T(128)S(6)} %select_n.233, s32[]{:T(128)S(6)} %select_n.234, s32[]{:T(128)S(6)} %select_n.235) | dynamic-update-slice | bytes 110596 | tf_op jit(solution)/shard_map/while/body/eval_jaxpr/dynamic_update_slice | solution.py:124
  637.4 18.9 %dynamic_update_slice.27 = f32[48,48,152]{2,1,0:T(8,128)S(1)} dynamic-update-slice(f32[48,48,152]{2,1,0:T(8,128)S(1)} %get-tuple-element.505, f32[24,24,24]{2,1,0:T(8,128)S(1)} %dynamic-slice_add_fusion.4, s32[]{:T(128)S(6)} %select_n.230, s32[]{:T(128)S(6)} %select_n.231, s32[]{:T(128)S(6)} %select_n.232) | dynamic-update-slice | bytes 110596 | tf_op jit(solution)/shard_map/while/body/eval_jaxpr/dynamic_update_slice | solution.py:124
  662.9 16.8 %dynamic_update_slice.28 = f32[48,48,152]{2,1,0:T(8,128)S(1)} dynamic-update-slice(f32[48,48,152]{2,1,0:T(8,128)S(1)} %dynamic_update_slice.27, f32[24,24,24]{2,1,0:T(8,128)S(1)} %dynamic-slice_add_fusion.5, s32[]{:T(128)S(6)} %select_n.233, s32[]{:T(128)S(6)} %select_n.234, s32[]{:T(128)S(6)} %select_n.235) | dynamic-update-slice | bytes 110596 | tf_op jit(solution)/shard_map/while/body/eval_jaxpr/dynamic_update_slice | solution.py:124
  687.6 11.6 dynamic_update_slice.27
  705.8 16.8 %dynamic_update_slice.28 = f32[48,48,152]{2,1,0:T(8,128)S(1)} dynamic-update-slice(f32[48,48,152]{2,1,0:T(8,128)S(1)} %dynamic_update_slice.27, f32[24,24,24]{2,1,0:T(8,128)S(1)} %dynamic-slice_add_fusion.5, s32[]{:T(128)S(6)} %select_n.233, s32[]{:T(128)S(6)} %select_n.234, s32[]{:T(128)S(6)} %select_n.235) | dynamic-update-slice | bytes 110596 | tf_op jit(solution)/shard_map/while/body/eval_jaxpr/dynamic_update_slice | solution.py:124
  730.4 19.7 %dynamic_update_slice.27 = f32[48,48,152]{2,1,0:T(8,128)S(1)} dynamic-update-slice(f32[48,48,152]{2,1,0:T(8,128)S(1)} %get-tuple-element.505, f32[24,24,24]{2,1,0:T(8,128)S(1)} %dynamic-slice_add_fusion.4, s32[]{:T(128)S(6)} %select_n.230, s32[]{:T(128)S(6)} %select_n.231, s32[]{:T(128)S(6)} %select_n.232) | dynamic-update-slice | bytes 110596 | tf_op jit(solution)/shard_map/while/body/eval_jaxpr/dynamic_update_slice | solution.py:124
  756.7 19.7 %dynamic_update_slice.28 = f32[48,48,152]{2,1,0:T(8,128)S(1)} dynamic-update-slice(f32[48,48,152]{2,1,0:T(8,128)S(1)} %dynamic_update_slice.27, f32[24,24,24]{2,1,0:T(8,128)S(1)} %dynamic-slice_add_fusion.5, s32[]{:T(128)S(6)} %select_n.233, s32[]{:T(128)S(6)} %select_n.234, s32[]{:T(128)S(6)} %select_n.235) | dynamic-update-slice | bytes 110596 | tf_op jit(solution)/shard_map/while/body/eval_jaxpr/dynamic_update_slice | solution.py:124
  784.3 20.5 %dynamic_update_slice.27 = f32[48,48,152]{2,1,0:T(8,128)S(1)} dynamic-update-slice(f32[48,48,152]{2,1,0:T(8,128)S(1)} %get-tuple-element.505, f32[24,24,24]{2,1,0:T(8,128)S(1)} %dynamic-slice_add_fusion.4, s32[]{:T(128)S(6)} %select_n.230, s32[]{:T(128)S(6)} %select_n.231, s32[]{:T(128)S(6)} %select_n.232) | dynamic-update-slice | bytes 110596 | tf_op jit(solution)/shard_map/while/body/eval_jaxpr/dynamic_update_slice | solution.py:124
  811.3 18.5 %dynamic_update_slice.28 = f32[48,48,152]{2,1,0:T(8,128)S(1)} dynamic-update-slice(f32[48,48,152]{2,1,0:T(8,128)S(1)} %dynamic_update_slice.27, f32[24,24,24]{2,1,0:T(8,128)S(1)} %dynamic-slice_add_fusion.5, s32[]{:T(128)S(6)} %select_n.233, s32[]{:T(128)S(6)} %select_n.234, s32[]{:T(128)S(6)} %select_n.235) | dynamic-update-slice | bytes 110596 | tf_op jit(solution)/shard_map/while/body/eval_jaxpr/dynamic_update_slice | solution.py:124
  837.7 18.1 %dynamic_update_slice.27 = f32[48,48,152]{2,1,0:T(8,128)S(1)} dynamic-update-slice(f32[48,48,152]{2,1,0:T(8,128)S(1)} %get-tuple-element.505, f32[24,24,24]{2,1,0:T(8,128)S(1)} %dynamic-slice_add_fusion.4, s32[]{:T(128)S(6)} %select_n.230, s32[]{:T(128)S(6)} %select_n.231, s32[]{:T(128)S(6)} %select_n.232) | dynamic-update-slice | bytes 110596 | tf_op jit(solution)/shard_map/while/body/eval_jaxpr/dynamic_update_slice | solution.py:124
  862.4 19.9 %dynamic_update_slice.28 = f32[48,48,152]{2,1,0:T(8,128)S(1)} dynamic-update-slice(f32[48,48,152]{2,1,0:T(8,128)S(1)} %dynamic_update_slice.27, f32[24,24,24]{2,1,0:T(8,128)S(1)} %dynamic-slice_add_fusion.5, s32[]{:T(128)S(6)} %select_n.233, s32[]{:T(128)S(6)} %select_n.234, s32[]{:T(128)S(6)} %select_n.235) | dynamic-update-slice | bytes 110596 | tf_op jit(solution)/shard_map/while/body/eval_jaxpr/dynamic_update_slice | solution.py:124
  883.6 6.9 scatter-add.4
  892.7 2.6 collective-permute-done
  896.5 4.0 collective-permute-start.1
  900.6 3.6 collective-permute-done.1
  905.0 87.0 %all-reduce.2.cloned.1.call-done = bf16[24,24,128]{2,1,0:T(8,128)(2,1)} async-done(((bf16[24,24,128]{2,1,0:T(8,128)(2,1)}), bf16[24,24,128]{2,1,0:T(8,128)(2,1)}) %all-reduce.2.cloned.1.call-update) | async-done | bytes 147472 | tf_op jit(solution)/shard_map/psum | solution.py:135
  1001.0 2.7 collective-permute-start.5
  1006.9 3.1 fusion.33
  1010.0 4.9 fusion.23
  1014.9 3.4 fusion.26
  1021.0 77.4 %while.39 = (s32[]{:T(128)}, bf16[6,12288]{1,0:T(8,128)(2,1)S(1)}, f32[6,8,12288]{2,0,1:T(8,128)}, f32[8,64]{1,0:T(8,128)S(1)}, f32[64]{0:T(128)S(1)}, /*index=5...) while((s32[]{:T(128)}, bf16[6,12288]{1,0:T(8,128)(2,1)S(1)}, ...), condition=%wide.region_6.7_spmd, body=%wide.region_5.6_spmd.sunk | while | flops 696791040 | bytes 14027641 | solution.py:80
  1023.3 2.7 fusion.161
  1026.0 3.8 fusion.162
  1036.2 2.7 fusion.161
  1038.9 3.8 fusion.162
  1049.1 2.7 fusion.161
  1051.8 3.8 fusion.162
  1062.0 2.7 fusion.161
  1064.7 3.8 fusion.162
  1074.9 2.7 fusion.161
  1077.6 3.8 fusion.162
  1087.8 2.7 fusion.161
  1090.5 3.8 fusion.162
  1098.7 3.8 collective-permute-start.6
  1104.6 3.3 collective-permute-start.7
  1107.9 4.9 collective-permute-done.7
  1112.8 211.0 %while.40 = (s32[]{:T(128)}, bf16[16,2,13824]{2,1,0:T(2,128)(2,1)S(1)}, s32[16,2,3]{2,1,0:T(2,128)}, bf16[48,48,152]{2,1,0:T(8,128)(2,1)S(1)}, s32[]{:T(128)}, /*index=5*/s32[]{:T(128)}, s32[]{:T(128)}, s32[]{:T(128)}) while((s32[]{:T(128)}, bf16[16,2,13824]{2,1,0:T(2,128)(2,1)S(1)}, s32[16,2,3]{2,1,0:T(2,128)}, ...), condition=%wide.region_8.9_spmd, body=%wide.region_7.8_spmd.sunk | while | flops 110612 | bytes 387489 | solution.py:157
  1323.9 32.4 %all_to_all.15 = bf16[16,2,13824]{2,1,0:T(2,128)(2,1)S(1)} all-to-all(bf16[16,2,13824]{2,1,0:T(2,128)(2,1)S(1)} %get-tuple-element.204), channel_id=1, replica_groups=mesh['gz'=16,'gy'=8,'orb'=2] {'gz'}, dimensions={0} | all-to-all | bytes 1769472 | tf_op jit(solution)/shard_map/all_to_all | solution.py:160
  (327 shorter events, 152.8 us)
Async XLA Ops:
  10.4 16.9 %all-to-all-start = ((bf16[16,2,3]{2,1,0:T(2,128)(2,1)}), bf16[16,2,3]{2,1,0:T(2,128)(2,1)S(1)}, u32[]{:S(2)}, u32[]{:S(2)}) async-start(bf16[16,2,3]{2,1,0:T(2,128)(2,1)} %bitcast.41), calls=%async_computation | async-start | bytes 16384 | tf_op jit(solution)/shard_map/all_to_all | solution.py:109
  21.8 11.6 copy-start.18
  27.3 29.5 %all-to-all-start.1 = ((bf16[16,2,13824]{2,1,0:T(2,128)(2,1)}), bf16[16,2,13824]{2,1,0:T(2,128)(2,1)}, u32[]{:S(2)}, u32[]{:S(2)}) async-start(bf16[16,2,13824]{2,1,0:T(2,128)(2,1)} %reshape.511), calls=%async_computation.1 | async-start | bytes 1769472 | tf_op jit(solution)/shard_map/all_to_all | solution.py:106
  32.0 960.0 %all-reduce.2.cloned.1.call-start = ((), (), s32[]{:S(2)}) async-start(), calls=%async_computation.3 | async-start | bytes 294912 | tf_op jit(solution)/shard_map/psum | solution.py:135
  37.5 19.6 %copy-start.15 = (s32[16,2,3]{2,1,0:T(2,128)}, s32[16,2,3]{2,1,0:T(2,128)S(1)}, u32[]{:S(2)}) copy-start(s32[16,2,3]{2,1,0:T(2,128)S(1)} %convert_convert_fusion) | copy-start | bytes 1156
  883.5 123.3 %copy-start.2 = (f32[128,128]{1,0:T(8,128)S(1)}, f32[128,128]{1,0:T(8,128)}, u32[]{:S(2)}) copy-start(f32[128,128]{1,0:T(8,128)} %compare_convert_fusion.12) | copy-start | bytes 196612
  883.5 123.2 %copy-start.3 = (f32[128,128]{1,0:T(8,128)S(1)}, f32[128,128]{1,0:T(8,128)}, u32[]{:S(2)}) copy-start(f32[128,128]{1,0:T(8,128)} %get-tuple-element.335) | copy-start | bytes 196612
  883.6 123.2 %copy-start.4 = (f32[128,128]{1,0:T(8,128)S(1)}, f32[128,128]{1,0:T(8,128)}, u32[]{:S(2)}) copy-start(f32[128,128]{1,0:T(8,128)} %get-tuple-element.336) | copy-start | bytes 196612
  883.6 123.2 %copy-start.5 = (f32[128,128]{1,0:T(8,128)S(1)}, f32[128,128]{1,0:T(8,128)}, u32[]{:S(2)}) copy-start(f32[128,128]{1,0:T(8,128)} %get-tuple-element.337) | copy-start | bytes 196612
  883.6 123.2 %copy-start.6 = (f32[128,128]{1,0:T(8,128)S(1)}, f32[128,128]{1,0:T(8,128)}, u32[]{:S(2)}) copy-start(f32[128,128]{1,0:T(8,128)} %get-tuple-element.338) | copy-start | bytes 196612
  883.6 123.2 %copy-start.7 = (f32[128,128]{1,0:T(8,128)S(1)}, f32[128,128]{1,0:T(8,128)}, u32[]{:S(2)}) copy-start(f32[128,128]{1,0:T(8,128)} %get-tuple-element.339) | copy-start | bytes 196612
  883.6 123.2 %copy-start.8 = (f32[128,128]{1,0:T(8,128)S(1)}, f32[128,128]{1,0:T(8,128)}, u32[]{:S(2)}) copy-start(f32[128,128]{1,0:T(8,128)} %get-tuple-element.340) | copy-start | bytes 196612
  883.6 123.2 %copy-start.9 = (f32[128,128]{1,0:T(8,128)S(1)}, f32[128,128]{1,0:T(8,128)}, u32[]{:S(2)}) copy-start(f32[128,128]{1,0:T(8,128)} %get-tuple-element.341) | copy-start | bytes 196612
  883.6 123.2 %copy-start.10 = (f32[128,128]{1,0:T(8,128)S(1)}, f32[128,128]{1,0:T(8,128)}, u32[]{:S(2)}) copy-start(f32[128,128]{1,0:T(8,128)} %get-tuple-element.342) | copy-start | bytes 196612
  891.7 3.7 collective-permute-start
  896.5 7.7 collective-permute-start.1
  992.8 3.3 collective-permute-start.2
  995.1 3.4 collective-permute-start.3
  998.5 6.9 collective-permute-start.4
  1001.0 5.8 collective-permute-start.5
  1006.8 3.2 copy-start.11
  1006.9 3.2 copy-start.12
  1006.9 3.2 copy-start.13
  1018.8 2.2 copy-start.14
  1018.8 2.2 copy-start.16
  1018.8 2.2 copy-start.17
  1018.8 2.2 copy-start.19
  1018.8 2.2 copy-start.20
  1098.6 14.2 %copy-start.1 = (bf16[24,24,128]{2,1,0:T(8,128)(2,1)}, bf16[24,24,128]{2,1,0:T(8,128)(2,1)S(1)}, u32[]{:S(2)}) copy-start(bf16[24,24,128]{2,1,0:T(8,128)(2,1)S(1)} %convert_element_type.308) | copy-start | bytes 442372
  1098.7 5.9 collective-permute-start.6
  1104.6 8.2 collective-permute-start.7
  1323.8 33.5 %copy-start = (bf16[16,24,576]{2,1,0:T(8,128)(2,1)S(1)}, bf16[16,24,576]{2,1,0:T(8,128)(2,1)}, u32[]{:S(2)}) copy-start(bf16[16,24,576]{2,1,0:T(8,128)(2,1)} %param.26) | copy-start | bytes 1327108
Sparse Core Ops, SparseCore 0:
  905.0 86.9 all-reduce.1
where the time goes:
time: 1370 us
  local copies, waits for them, and re-layouts  685 us (50%)
  loops' own time  365 us (27%)
  waiting for transfers between devices  128 us (9%)
  matrix products  65.3 us (5%)
  other arithmetic  42 us (3%)
  starting transfers between devices  33.3 us (2%)
  blocking collectives  32.4 us (2%)
  between operations  14.5 us (1%)
    dynamic_update_slice x32, local copies, waits for them, and re-layouts, deposit(): grid = lax.dynamic_update_slice(grid, region + piece, start)  595 us
    another operation x1, loops' own time, local(): lax.fori_loop(0, slab_count, deposit, jnp.zeros((CZ + BOX, CY + BOX, NX +...  189 us
    another operation x1, loops' own time, local(): windows = lax.map(cut, offsets)  176 us
    psum x1, waiting for transfers between devices, local(): density = lax.psum(tile.astype(jnp.bfloat16), 'orb').astype(jnp.float32)  87 us
    all_to_all x1, blocking collectives, local(): lax.all_to_all(for_sending(windows), 'gz', split_axis=0, concat_axis=0, t...  32.4 us
  transfers between devices with their start and end apart: 11, of which 11 were waited for; matrix products, arithmetic and copies ran while one was open for 1% of the time, Pallas kernels for 0%

commit v1 on v0

--- a/solution.py
+++ b/solution.py
@@ -12,6 +12,7 @@
 CAP = 2
 CELL_BLOCK = 12288
 exact_mode = lax.Precision.HIGHEST
+start_task = lambda unit, shard_axis: jnp.sum(lax.all_gather(unit, shard_axis), axis=0)
 
 
 def shifted(x, axis, by):
@@ -132,7 +133,7 @@
     core = extended[:CZ].at[:BOX].add(from_below)
     from_left = shifted(core[:, CY:].astype(jnp.bfloat16), "gy", 1).astype(jnp.float32)
     tile = core[:, :CY].at[:, :BOX].add(from_left)
-    density = lax.psum(tile.astype(jnp.bfloat16), "orb").astype(jnp.float32)
+    density = start_task(tile.astype(jnp.bfloat16), shard_axis="orb").astype(jnp.float32)
     padded = extended_2(density.astype(jnp.bfloat16), (("gz", 0), ("gy", 1)), RAD).astype(
         density.dtype
     )

time: 1370 us -> 1320 us (0.964)
  waiting for transfers between devices: 128 us -> 33.3 us
  starting transfers between devices: 33.3 us -> 81.7 us
  blocking collectives: 32.4 us -> 47.1 us
    psum x1 -> x0, waiting for transfers between devices: 87 us -> none  [local(): density = lax.psum(tile.astype(jnp.bfloat16), 'orb').astype(jnp.float32)]
    ppermute x4, starting transfers between devices: 11.1 us -> 36.4 us  [shifted(): return lax.ppermute(x, axis, [(i, (i + by) % count) for i in range(count)])]
    ppermute x2, starting transfers between devices: 2.68 us -> 22.1 us  [extended_2(): lax.ppermute(head, axis, [((i + 1) % count, i) for i in range(count)])]
    all_gather x0 -> x1, blocking collectives: none -> 14.3 us  [lax.all_gather(unit, shard_axis)]
  transfers between devices with their start and end apart: 11 -> 10, of which waited for: 11 -> 9; matrix products, arithmetic and copies ran while one was open for 1% -> 1% of each run, Pallas kernels for 0% -> 0%
where the time goes in v1:
time: 1320 us; the launch traced here: 1310 us
  local copies, waits for them, and re-layouts  683 us (52%)
  loops' own time  356 us (27%)
  starting transfers between devices  81.7 us (6%)
  matrix products  65.3 us (5%)
  blocking collectives  47.1 us (4%)
  other arithmetic  42.6 us (3%)
  waiting for transfers between devices  33.3 us (3%)
    dynamic_update_slice x32, local copies, waits for them, and re-layouts, deposit(): grid = lax.dynamic_update_slice(grid, region + piece, start)  595 us
    another operation x1, loops' own time, local(): lax.fori_loop(0, slab_count, deposit, jnp.zeros((CZ + BOX, CY + BOX, NX +...  180 us
    another operation x1, loops' own time, local(): windows = lax.map(cut, offsets)  176 us
    ppermute x4, starting transfers between devices, shifted(): return lax.ppermute(x, axis, [(i, (i + by) % count) for i in range(count)])  36.4 us
    all_to_all x1, blocking collectives, local(): lax.all_to_all(for_sending(windows), 'gz', split_axis=0, concat_axis=0, t...  32.9 us
  transfers between devices with their start and end apart: 10, of which 9 were waited for; matrix products, arithmetic and copies ran while one was open for 1% of the time, Pallas kernels for 0%

profile of v1, /device:TPU:1, one launch (start us, length us, event | category | flops | bytes accessed | tf_op | source)
XLA Modules:
  0.0 1310.4 jit_solution(10331546269419292402)
XLA Ops:
  3.9 10.0 all-to-all-start
  20.8 5.0 all-to-all-start.1
  31.4 19.1 %all-to-all-done.1 = bf16[16,2,13824]{2,1,0:T(2,128)(2,1)} async-done(((bf16[16,2,13824]{2,1,0:T(2,128)(2,1)}), bf16[16,2,13824]{2,1,0:T(2,128)(2,1)}, u32[]{:S(2)}, u32[]{:S(2)}) %all-to-all-start.1) | async-done | bytes 884768 | tf_op jit(solution)/shard_map/all_to_all | solution.py:107
  50.8 816.2 %while.38 = (s32[]{:T(128)}, f32[48,48,152]{2,1,0:T(8,128)S(1)}, s32[16,2,3]{0,1,2:T(2,128)S(1)}, bf16[16,2,13824]{2,1,0:T(2,128)(2,1)}, s32[]{:T(128)}, /*index=5*/s32[]{:T(128)}, s32[]{:T(128)}, s32[]{:T(128)}) while((s32[]{:T(128)}, f32[48,48,152]{2,1,0:T(8,128)S(1)}, s32[16,2,3]{0,1,2:T(2,128)S(1)}, bf16[16,2,13824]{2,1,0:T(2,128)(2,1)}, ...), condition=%wide.region_3.4_spmd, body=%wide.region_2.3_spmd.sunk | while | flops 55316 | bytes 940409 | solution.py:128
  58.5 16.9 %dynamic_update_slice.27 = f32[48,48,152]{2,1,0:T(8,128)S(1)} dynamic-update-slice(f32[48,48,152]{2,1,0:T(8,128)S(1)} %get-tuple-element.505, f32[24,24,24]{2,1,0:T(8,128)S(1)} %dynamic-slice_add_fusion.4, s32[]{:T(128)S(6)} %select_n.230, s32[]{:T(128)S(6)} %select_n.231, s32[]{:T(128)S(6)} %select_n.232) | dynamic-update-slice | bytes 110596 | tf_op jit(solution)/shard_map/while/body/eval_jaxpr/dynamic_update_slice | solution.py:125
  81.5 16.8 %dynamic_update_slice.28 = f32[48,48,152]{2,1,0:T(8,128)S(1)} dynamic-update-slice(f32[48,48,152]{2,1,0:T(8,128)S(1)} %dynamic_update_slice.27, f32[24,24,24]{2,1,0:T(8,128)S(1)} %dynamic-slice_add_fusion.5, s32[]{:T(128)S(6)} %select_n.233, s32[]{:T(128)S(6)} %select_n.234, s32[]{:T(128)S(6)} %select_n.235) | dynamic-update-slice | bytes 110596 | tf_op jit(solution)/shard_map/while/body/eval_jaxpr/dynamic_update_slice | solution.py:125
  106.0 23.0 %dynamic_update_slice.27 = f32[48,48,152]{2,1,0:T(8,128)S(1)} dynamic-update-slice(f32[48,48,152]{2,1,0:T(8,128)S(1)} %get-tuple-element.505, f32[24,24,24]{2,1,0:T(8,128)S(1)} %dynamic-slice_add_fusion.4, s32[]{:T(128)S(6)} %select_n.230, s32[]{:T(128)S(6)} %select_n.231, s32[]{:T(128)S(6)} %select_n.232) | dynamic-update-slice | bytes 110596 | tf_op jit(solution)/shard_map/while/body/eval_jaxpr/dynamic_update_slice | solution.py:125
  135.1 20.9 %dynamic_update_slice.28 = f32[48,48,152]{2,1,0:T(8,128)S(1)} dynamic-update-slice(f32[48,48,152]{2,1,0:T(8,128)S(1)} %dynamic_update_slice.27, f32[24,24,24]{2,1,0:T(8,128)S(1)} %dynamic-slice_add_fusion.5, s32[]{:T(128)S(6)} %select_n.233, s32[]{:T(128)S(6)} %select_n.234, s32[]{:T(128)S(6)} %select_n.235) | dynamic-update-slice | bytes 110596 | tf_op jit(solution)/shard_map/while/body/eval_jaxpr/dynamic_update_slice | solution.py:125
  163.8 22.8 %dynamic_update_slice.27 = f32[48,48,152]{2,1,0:T(8,128)S(1)} dynamic-update-slice(f32[48,48,152]{2,1,0:T(8,128)S(1)} %get-tuple-element.505, f32[24,24,24]{2,1,0:T(8,128)S(1)} %dynamic-slice_add_fusion.4, s32[]{:T(128)S(6)} %select_n.230, s32[]{:T(128)S(6)} %select_n.231, s32[]{:T(128)S(6)} %select_n.232) | dynamic-update-slice | bytes 110596 | tf_op jit(solution)/shard_map/while/body/eval_jaxpr/dynamic_update_slice | solution.py:125
  192.7 16.8 %dynamic_update_slice.28 = f32[48,48,152]{2,1,0:T(8,128)S(1)} dynamic-update-slice(f32[48,48,152]{2,1,0:T(8,128)S(1)} %dynamic_update_slice.27, f32[24,24,24]{2,1,0:T(8,128)S(1)} %dynamic-slice_add_fusion.5, s32[]{:T(128)S(6)} %select_n.233, s32[]{:T(128)S(6)} %select_n.234, s32[]{:T(128)S(6)} %select_n.235) | dynamic-update-slice | bytes 110596 | tf_op jit(solution)/shard_map/while/body/eval_jaxpr/dynamic_update_slice | solution.py:125
  217.2 20.7 %dynamic_update_slice.27 = f32[48,48,152]{2,1,0:T(8,128)S(1)} dynamic-update-slice(f32[48,48,152]{2,1,0:T(8,128)S(1)} %get-tuple-element.505, f32[24,24,24]{2,1,0:T(8,128)S(1)} %dynamic-slice_add_fusion.4, s32[]{:T(128)S(6)} %select_n.230, s32[]{:T(128)S(6)} %select_n.231, s32[]{:T(128)S(6)} %select_n.232) | dynamic-update-slice | bytes 110596 | tf_op jit(solution)/shard_map/while/body/eval_jaxpr/dynamic_update_slice | solution.py:125
  244.0 16.8 %dynamic_update_slice.28 = f32[48,48,152]{2,1,0:T(8,128)S(1)} dynamic-update-slice(f32[48,48,152]{2,1,0:T(8,128)S(1)} %dynamic_update_slice.27, f32[24,24,24]{2,1,0:T(8,128)S(1)} %dynamic-slice_add_fusion.5, s32[]{:T(128)S(6)} %select_n.233, s32[]{:T(128)S(6)} %select_n.234, s32[]{:T(128)S(6)} %select_n.235) | dynamic-update-slice | bytes 110596 | tf_op jit(solution)/shard_map/while/body/eval_jaxpr/dynamic_update_slice | solution.py:125
  268.6 19.7 %dynamic_update_slice.27 = f32[48,48,152]{2,1,0:T(8,128)S(1)} dynamic-update-slice(f32[48,48,152]{2,1,0:T(8,128)S(1)} %get-tuple-element.505, f32[24,24,24]{2,1,0:T(8,128)S(1)} %dynamic-slice_add_fusion.4, s32[]{:T(128)S(6)} %select_n.230, s32[]{:T(128)S(6)} %select_n.231, s32[]{:T(128)S(6)} %select_n.232) | dynamic-update-slice | bytes 110596 | tf_op jit(solution)/shard_map/while/body/eval_jaxpr/dynamic_update_slice | solution.py:125
  294.4 16.8 %dynamic_update_slice.28 = f32[48,48,152]{2,1,0:T(8,128)S(1)} dynamic-update-slice(f32[48,48,152]{2,1,0:T(8,128)S(1)} %dynamic_update_slice.27, f32[24,24,24]{2,1,0:T(8,128)S(1)} %dynamic-slice_add_fusion.5, s32[]{:T(128)S(6)} %select_n.233, s32[]{:T(128)S(6)} %select_n.234, s32[]{:T(128)S(6)} %select_n.235) | dynamic-update-slice | bytes 110596 | tf_op jit(solution)/shard_map/while/body/eval_jaxpr/dynamic_update_slice | solution.py:125
  319.0 16.8 %dynamic_update_slice.27 = f32[48,48,152]{2,1,0:T(8,128)S(1)} dynamic-update-slice(f32[48,48,152]{2,1,0:T(8,128)S(1)} %get-tuple-element.505, f32[24,24,24]{2,1,0:T(8,128)S(1)} %dynamic-slice_add_fusion.4, s32[]{:T(128)S(6)} %select_n.230, s32[]{:T(128)S(6)} %select_n.231, s32[]{:T(128)S(6)} %select_n.232) | dynamic-update-slice | bytes 110596 | tf_op jit(solution)/shard_map/while/body/eval_jaxpr/dynamic_update_slice | solution.py:125
  341.8 16.8 %dynamic_update_slice.28 = f32[48,48,152]{2,1,0:T(8,128)S(1)} dynamic-update-slice(f32[48,48,152]{2,1,0:T(8,128)S(1)} %dynamic_update_slice.27, f32[24,24,24]{2,1,0:T(8,128)S(1)} %dynamic-slice_add_fusion.5, s32[]{:T(128)S(6)} %select_n.233, s32[]{:T(128)S(6)} %select_n.234, s32[]{:T(128)S(6)} %select_n.235) | dynamic-update-slice | bytes 110596 | tf_op jit(solution)/shard_map/while/body/eval_jaxpr/dynamic_update_slice | solution.py:125
  366.4 22.1 %dynamic_update_slice.27 = f32[48,48,152]{2,1,0:T(8,128)S(1)} dynamic-update-slice(f32[48,48,152]{2,1,0:T(8,128)S(1)} %get-tuple-element.505, f32[24,24,24]{2,1,0:T(8,128)S(1)} %dynamic-slice_add_fusion.4, s32[]{:T(128)S(6)} %select_n.230, s32[]{:T(128)S(6)} %select_n.231, s32[]{:T(128)S(6)} %select_n.232) | dynamic-update-slice | bytes 110596 | tf_op jit(solution)/shard_map/while/body/eval_jaxpr/dynamic_update_slice | solution.py:125
  394.6 16.8 %dynamic_update_slice.28 = f32[48,48,152]{2,1,0:T(8,128)S(1)} dynamic-update-slice(f32[48,48,152]{2,1,0:T(8,128)S(1)} %dynamic_update_slice.27, f32[24,24,24]{2,1,0:T(8,128)S(1)} %dynamic-slice_add_fusion.5, s32[]{:T(128)S(6)} %select_n.233, s32[]{:T(128)S(6)} %select_n.234, s32[]{:T(128)S(6)} %select_n.235) | dynamic-update-slice | bytes 110596 | tf_op jit(solution)/shard_map/while/body/eval_jaxpr/dynamic_update_slice | solution.py:125
  419.1 21.6 %dynamic_update_slice.27 = f32[48,48,152]{2,1,0:T(8,128)S(1)} dynamic-update-slice(f32[48,48,152]{2,1,0:T(8,128)S(1)} %get-tuple-element.505, f32[24,24,24]{2,1,0:T(8,128)S(1)} %dynamic-slice_add_fusion.4, s32[]{:T(128)S(6)} %select_n.230, s32[]{:T(128)S(6)} %select_n.231, s32[]{:T(128)S(6)} %select_n.232) | dynamic-update-slice | bytes 110596 | tf_op jit(solution)/shard_map/while/body/eval_jaxpr/dynamic_update_slice | solution.py:125
  446.8 19.7 %dynamic_update_slice.28 = f32[48,48,152]{2,1,0:T(8,128)S(1)} dynamic-update-slice(f32[48,48,152]{2,1,0:T(8,128)S(1)} %dynamic_update_slice.27, f32[24,24,24]{2,1,0:T(8,128)S(1)} %dynamic-slice_add_fusion.5, s32[]{:T(128)S(6)} %select_n.233, s32[]{:T(128)S(6)} %select_n.234, s32[]{:T(128)S(6)} %select_n.235) | dynamic-update-slice | bytes 110596 | tf_op jit(solution)/shard_map/while/body/eval_jaxpr/dynamic_update_slice | solution.py:125
  474.3 17.9 %dynamic_update_slice.27 = f32[48,48,152]{2,1,0:T(8,128)S(1)} dynamic-update-slice(f32[48,48,152]{2,1,0:T(8,128)S(1)} %get-tuple-element.505, f32[24,24,24]{2,1,0:T(8,128)S(1)} %dynamic-slice_add_fusion.4, s32[]{:T(128)S(6)} %select_n.230, s32[]{:T(128)S(6)} %select_n.231, s32[]{:T(128)S(6)} %select_n.232) | dynamic-update-slice | bytes 110596 | tf_op jit(solution)/shard_map/while/body/eval_jaxpr/dynamic_update_slice | solution.py:125
  498.3 19.5 %dynamic_update_slice.28 = f32[48,48,152]{2,1,0:T(8,128)S(1)} dynamic-update-slice(f32[48,48,152]{2,1,0:T(8,128)S(1)} %dynamic_update_slice.27, f32[24,24,24]{2,1,0:T(8,128)S(1)} %dynamic-slice_add_fusion.5, s32[]{:T(128)S(6)} %select_n.233, s32[]{:T(128)S(6)} %select_n.234, s32[]{:T(128)S(6)} %select_n.235) | dynamic-update-slice | bytes 110596 | tf_op jit(solution)/shard_map/while/body/eval_jaxpr/dynamic_update_slice | solution.py:125
  525.5 18.6 %dynamic_update_slice.27 = f32[48,48,152]{2,1,0:T(8,128)S(1)} dynamic-update-slice(f32[48,48,152]{2,1,0:T(8,128)S(1)} %get-tuple-element.505, f32[24,24,24]{2,1,0:T(8,128)S(1)} %dynamic-slice_add_fusion.4, s32[]{:T(128)S(6)} %select_n.230, s32[]{:T(128)S(6)} %select_n.231, s32[]{:T(128)S(6)} %select_n.232) | dynamic-update-slice | bytes 110596 | tf_op jit(solution)/shard_map/while/body/eval_jaxpr/dynamic_update_slice | solution.py:125
  550.2 16.8 %dynamic_update_slice.28 = f32[48,48,152]{2,1,0:T(8,128)S(1)} dynamic-update-slice(f32[48,48,152]{2,1,0:T(8,128)S(1)} %dynamic_update_slice.27, f32[24,24,24]{2,1,0:T(8,128)S(1)} %dynamic-slice_add_fusion.5, s32[]{:T(128)S(6)} %select_n.233, s32[]{:T(128)S(6)} %select_n.234, s32[]{:T(128)S(6)} %select_n.235) | dynamic-update-slice | bytes 110596 | tf_op jit(solution)/shard_map/while/body/eval_jaxpr/dynamic_update_slice | solution.py:125
  574.8 19.4 %dynamic_update_slice.27 = f32[48,48,152]{2,1,0:T(8,128)S(1)} dynamic-update-slice(f32[48,48,152]{2,1,0:T(8,128)S(1)} %get-tuple-element.505, f32[24,24,24]{2,1,0:T(8,128)S(1)} %dynamic-slice_add_fusion.4, s32[]{:T(128)S(6)} %select_n.230, s32[]{:T(128)S(6)} %select_n.231, s32[]{:T(128)S(6)} %select_n.232) | dynamic-update-slice | bytes 110596 | tf_op jit(solution)/shard_map/while/body/eval_jaxpr/dynamic_update_slice | solution.py:125
  600.3 16.8 %dynamic_update_slice.28 = f32[48,48,152]{2,1,0:T(8,128)S(1)} dynamic-update-slice(f32[48,48,152]{2,1,0:T(8,128)S(1)} %dynamic_update_slice.27, f32[24,24,24]{2,1,0:T(8,128)S(1)} %dynamic-slice_add_fusion.5, s32[]{:T(128)S(6)} %select_n.233, s32[]{:T(128)S(6)} %select_n.234, s32[]{:T(128)S(6)} %select_n.235) | dynamic-update-slice | bytes 110596 | tf_op jit(solution)/shard_map/while/body/eval_jaxpr/dynamic_update_slice | solution.py:125
  624.9 18.9 %dynamic_update_slice.27 = f32[48,48,152]{2,1,0:T(8,128)S(1)} dynamic-update-slice(f32[48,48,152]{2,1,0:T(8,128)S(1)} %get-tuple-element.505, f32[24,24,24]{2,1,0:T(8,128)S(1)} %dynamic-slice_add_fusion.4, s32[]{:T(128)S(6)} %select_n.230, s32[]{:T(128)S(6)} %select_n.231, s32[]{:T(128)S(6)} %select_n.232) | dynamic-update-slice | bytes 110596 | tf_op jit(solution)/shard_map/while/body/eval_jaxpr/dynamic_update_slice | solution.py:125
  649.9 16.8 %dynamic_update_slice.28 = f32[48,48,152]{2,1,0:T(8,128)S(1)} dynamic-update-slice(f32[48,48,152]{2,1,0:T(8,128)S(1)} %dynamic_update_slice.27, f32[24,24,24]{2,1,0:T(8,128)S(1)} %dynamic-slice_add_fusion.5, s32[]{:T(128)S(6)} %select_n.233, s32[]{:T(128)S(6)} %select_n.234, s32[]{:T(128)S(6)} %select_n.235) | dynamic-update-slice | bytes 110596 | tf_op jit(solution)/shard_map/while/body/eval_jaxpr/dynamic_update_slice | solution.py:125
  674.4 11.6 dynamic_update_slice.27
  692.2 16.8 %dynamic_update_slice.28 = f32[48,48,152]{2,1,0:T(8,128)S(1)} dynamic-update-slice(f32[48,48,152]{2,1,0:T(8,128)S(1)} %dynamic_update_slice.27, f32[24,24,24]{2,1,0:T(8,128)S(1)} %dynamic-slice_add_fusion.5, s32[]{:T(128)S(6)} %select_n.233, s32[]{:T(128)S(6)} %select_n.234, s32[]{:T(128)S(6)} %select_n.235) | dynamic-update-slice | bytes 110596 | tf_op jit(solution)/shard_map/while/body/eval_jaxpr/dynamic_update_slice | solution.py:125
  716.7 19.7 %dynamic_update_slice.27 = f32[48,48,152]{2,1,0:T(8,128)S(1)} dynamic-update-slice(f32[48,48,152]{2,1,0:T(8,128)S(1)} %get-tuple-element.505, f32[24,24,24]{2,1,0:T(8,128)S(1)} %dynamic-slice_add_fusion.4, s32[]{:T(128)S(6)} %select_n.230, s32[]{:T(128)S(6)} %select_n.231, s32[]{:T(128)S(6)} %select_n.232) | dynamic-update-slice | bytes 110596 | tf_op jit(solution)/shard_map/while/body/eval_jaxpr/dynamic_update_slice | solution.py:125
  742.6 19.7 %dynamic_update_slice.28 = f32[48,48,152]{2,1,0:T(8,128)S(1)} dynamic-update-slice(f32[48,48,152]{2,1,0:T(8,128)S(1)} %dynamic_update_slice.27, f32[24,24,24]{2,1,0:T(8,128)S(1)} %dynamic-slice_add_fusion.5, s32[]{:T(128)S(6)} %select_n.233, s32[]{:T(128)S(6)} %select_n.234, s32[]{:T(128)S(6)} %select_n.235) | dynamic-update-slice | bytes 110596 | tf_op jit(solution)/shard_map/while/body/eval_jaxpr/dynamic_update_slice | solution.py:125
  770.1 20.5 %dynamic_update_slice.27 = f32[48,48,152]{2,1,0:T(8,128)S(1)} dynamic-update-slice(f32[48,48,152]{2,1,0:T(8,128)S(1)} %get-tuple-element.505, f32[24,24,24]{2,1,0:T(8,128)S(1)} %dynamic-slice_add_fusion.4, s32[]{:T(128)S(6)} %select_n.230, s32[]{:T(128)S(6)} %select_n.231, s32[]{:T(128)S(6)} %select_n.232) | dynamic-update-slice | bytes 110596 | tf_op jit(solution)/shard_map/while/body/eval_jaxpr/dynamic_update_slice | solution.py:125
  796.6 18.5 %dynamic_update_slice.28 = f32[48,48,152]{2,1,0:T(8,128)S(1)} dynamic-update-slice(f32[48,48,152]{2,1,0:T(8,128)S(1)} %dynamic_update_slice.27, f32[24,24,24]{2,1,0:T(8,128)S(1)} %dynamic-slice_add_fusion.5, s32[]{:T(128)S(6)} %select_n.233, s32[]{:T(128)S(6)} %select_n.234, s32[]{:T(128)S(6)} %select_n.235) | dynamic-update-slice | bytes 110596 | tf_op jit(solution)/shard_map/while/body/eval_jaxpr/dynamic_update_slice | solution.py:125
  822.9 18.1 %dynamic_update_slice.27 = f32[48,48,152]{2,1,0:T(8,128)S(1)} dynamic-update-slice(f32[48,48,152]{2,1,0:T(8,128)S(1)} %get-tuple-element.505, f32[24,24,24]{2,1,0:T(8,128)S(1)} %dynamic-slice_add_fusion.4, s32[]{:T(128)S(6)} %select_n.230, s32[]{:T(128)S(6)} %select_n.231, s32[]{:T(128)S(6)} %select_n.232) | dynamic-update-slice | bytes 110596 | tf_op jit(solution)/shard_map/while/body/eval_jaxpr/dynamic_update_slice | solution.py:125
  847.1 19.9 %dynamic_update_slice.28 = f32[48,48,152]{2,1,0:T(8,128)S(1)} dynamic-update-slice(f32[48,48,152]{2,1,0:T(8,128)S(1)} %dynamic_update_slice.27, f32[24,24,24]{2,1,0:T(8,128)S(1)} %dynamic-slice_add_fusion.5, s32[]{:T(128)S(6)} %select_n.233, s32[]{:T(128)S(6)} %select_n.234, s32[]{:T(128)S(6)} %select_n.235) | dynamic-update-slice | bytes 110596 | tf_op jit(solution)/shard_map/while/body/eval_jaxpr/dynamic_update_slice | solution.py:125
  868.4 6.9 scatter-add.4
  881.2 4.0 collective-permute-start.1
  885.3 3.6 collective-permute-done.1
  889.0 14.3 %all-gather = bf16[48,24,128]{2,1,0:T(8,128)(2,1)S(1)} all-gather(bf16[24,24,128]{2,1,0:T(8,128)(2,1)S(1)} %fusion.68), channel_id=2, replica_groups=mesh['gz'=16,'gy'=8,'orb'=2] {'orb'}, dimensions={0}, use_global_device_ids=true | all-gather | bytes 442368 | tf_op jit(solution)/shard_map/all_gather | solution.py:15
  903.3 4.2 collective-permute-start.2
  907.5 15.5 %collective-permute-start.3 = (bf16[6,24,128]{2,1,0:T(8,128)(2,1)S(1)}, bf16[6,24,128]{2,1,0:T(8,128)(2,1)S(1)}, u32[]{:S(2)}, u32[]{:S(2)}) collective-permute-start(bf16[6,24,128]{2,1,0:T(8,128)(2,1)S(1)} %get-tuple-element.319), channel_id=1, source_target_pairs={{16,0},{32,16},{48,32},{64,48},{80,64},{96,80},{112,96},{128,112},... | collective-permute-start | bytes 110600 | tf_op jit(solution)/shard_map/ppermute | solution.py:32
  924.0 4.0 collective-permute-start.4
  927.9 6.6 collective-permute-start.5
  936.2 3.1 fusion.33
  939.3 4.9 fusion.23
  944.2 3.4 fusion.26
  950.4 77.4 %while.39 = (s32[]{:T(128)}, bf16[6,12288]{1,0:T(8,128)(2,1)S(1)}, f32[6,8,12288]{2,0,1:T(8,128)}, f32[8,64]{1,0:T(8,128)S(1)}, f32[64]{0:T(128)S(1)}, /*index=5...) while((s32[]{:T(128)}, bf16[6,12288]{1,0:T(8,128)(2,1)S(1)}, ...), condition=%wide.region_6.7_spmd, body=%wide.region_5.6_spmd.sunk | while | flops 696791040 | bytes 14027641 | solution.py:81
  952.7 2.7 fusion.164
  955.4 3.8 fusion.165
  965.6 2.7 fusion.164
  968.3 3.8 fusion.165
  978.5 2.7 fusion.164
  981.2 3.8 fusion.165
  991.4 2.7 fusion.164
  994.1 3.8 fusion.165
  1004.3 2.7 fusion.164
  1007.0 3.8 fusion.165
  1017.2 2.7 fusion.164
  1019.8 3.8 fusion.165
  1028.0 26.2 %collective-permute-start.6 = (bf16[24,24,128]{2,1,0:T(8,128)(2,1)S(1)}, bf16[24,24,128]{2,1,0:T(8,128)(2,1)S(1)}, u32[]{:S(2)}, u32[]{:S(2)}) collective-permute-start(bf16[24,24,128]{2,1,0:T(8,128)(2,1)S(1)} %convert_element_type.310), channel_id=1, source_target_pairs={{0,14},{2,0},{4,2},{6,4},{8,6},{10,8},{12,10},{14,12},{1,15},{3,1}... | collective-permute-start | bytes 442376 | tf_op jit(solution)/shard_map/ppermute | solution.py:20
  1056.3 6.2 collective-permute-start.7
  1063.8 211.3 %while.40 = (s32[]{:T(128)}, bf16[16,2,13824]{2,1,0:T(2,128)(2,1)S(1)}, s32[16,2,3]{2,1,0:T(2,128)}, bf16[48,48,152]{2,1,0:T(8,128)(2,1)S(1)}, s32[]{:T(128)}, /*index=5*/s32[]{:T(128)}, s32[]{:T(128)}, s32[]{:T(128)}) while((s32[]{:T(128)}, bf16[16,2,13824]{2,1,0:T(2,128)(2,1)S(1)}, s32[16,2,3]{2,1,0:T(2,128)}, ...), condition=%wide.region_8.9_spmd, body=%wide.region_7.8_spmd.sunk | while | flops 110612 | bytes 387489 | solution.py:158
  1275.2 32.9 %all_to_all.15 = bf16[16,2,13824]{2,1,0:T(2,128)(2,1)S(1)} all-to-all(bf16[16,2,13824]{2,1,0:T(2,128)(2,1)S(1)} %get-tuple-element.204), channel_id=1, replica_groups=mesh['gz'=16,'gy'=8,'orb'=2] {'gz'}, dimensions={0} | all-to-all | bytes 1769472 | tf_op jit(solution)/shard_map/all_to_all | solution.py:161
  (331 shorter events, 149.6 us)
Async XLA Ops:
  3.9 16.9 %all-to-all-start = ((bf16[16,2,3]{2,1,0:T(2,128)(2,1)}), bf16[16,2,3]{2,1,0:T(2,128)(2,1)S(1)}, u32[]{:S(2)}, u32[]{:S(2)}) async-start(bf16[16,2,3]{2,1,0:T(2,128)(2,1)} %bitcast.41), calls=%async_computation | async-start | bytes 16384 | tf_op jit(solution)/shard_map/all_to_all | solution.py:110
  15.8 10.6 copy-start.22
  20.8 29.7 %all-to-all-start.1 = ((bf16[16,2,13824]{2,1,0:T(2,128)(2,1)}), bf16[16,2,13824]{2,1,0:T(2,128)(2,1)}, u32[]{:S(2)}, u32[]{:S(2)}) async-start(bf16[16,2,13824]{2,1,0:T(2,128)(2,1)} %reshape.511), calls=%async_computation.1 | async-start | bytes 1769472 | tf_op jit(solution)/shard_map/all_to_all | solution.py:107
  31.3 19.5 %copy-start.19 = (s32[16,2,3]{2,1,0:T(2,128)}, s32[16,2,3]{2,1,0:T(2,128)S(1)}, u32[]{:S(2)}) copy-start(s32[16,2,3]{2,1,0:T(2,128)S(1)} %convert_convert_fusion) | copy-start | bytes 1156
  868.3 67.8 %copy-start.2 = (f32[128,128]{1,0:T(8,128)S(1)}, f32[128,128]{1,0:T(8,128)}, u32[]{:S(2)}) copy-start(f32[128,128]{1,0:T(8,128)} %compare_convert_fusion.12) | copy-start | bytes 196612
  868.3 67.7 %copy-start.3 = (f32[128,128]{1,0:T(8,128)S(1)}, f32[128,128]{1,0:T(8,128)}, u32[]{:S(2)}) copy-start(f32[128,128]{1,0:T(8,128)} %get-tuple-element.335) | copy-start | bytes 196612
  868.3 67.7 %copy-start.4 = (f32[128,128]{1,0:T(8,128)S(1)}, f32[128,128]{1,0:T(8,128)}, u32[]{:S(2)}) copy-start(f32[128,128]{1,0:T(8,128)} %get-tuple-element.336) | copy-start | bytes 196612
  868.3 67.7 %copy-start.5 = (f32[128,128]{1,0:T(8,128)S(1)}, f32[128,128]{1,0:T(8,128)}, u32[]{:S(2)}) copy-start(f32[128,128]{1,0:T(8,128)} %get-tuple-element.337) | copy-start | bytes 196612
  868.3 67.7 %copy-start.6 = (f32[128,128]{1,0:T(8,128)S(1)}, f32[128,128]{1,0:T(8,128)}, u32[]{:S(2)}) copy-start(f32[128,128]{1,0:T(8,128)} %get-tuple-element.338) | copy-start | bytes 196612
  868.3 67.7 %copy-start.7 = (f32[128,128]{1,0:T(8,128)S(1)}, f32[128,128]{1,0:T(8,128)}, u32[]{:S(2)}) copy-start(f32[128,128]{1,0:T(8,128)} %get-tuple-element.339) | copy-start | bytes 196612
  868.3 67.7 %copy-start.8 = (f32[128,128]{1,0:T(8,128)S(1)}, f32[128,128]{1,0:T(8,128)}, u32[]{:S(2)}) copy-start(f32[128,128]{1,0:T(8,128)} %get-tuple-element.340) | copy-start | bytes 196612
  868.3 67.7 %copy-start.9 = (f32[128,128]{1,0:T(8,128)S(1)}, f32[128,128]{1,0:T(8,128)}, u32[]{:S(2)}) copy-start(f32[128,128]{1,0:T(8,128)} %get-tuple-element.341) | copy-start | bytes 196612
  868.3 67.7 %copy-start.10 = (f32[128,128]{1,0:T(8,128)S(1)}, f32[128,128]{1,0:T(8,128)}, u32[]{:S(2)}) copy-start(f32[128,128]{1,0:T(8,128)} %get-tuple-element.342) | copy-start | bytes 196612
  868.4 67.7 %copy-start.11 = (f32[128,128]{1,0:T(8,128)S(1)}, f32[128,128]{1,0:T(8,128)}, u32[]{:S(2)}) copy-start(f32[128,128]{1,0:T(8,128)} %get-tuple-element.343) | copy-start | bytes 196612
  868.4 67.7 %copy-start.12 = (f32[128,128]{1,0:T(8,128)S(1)}, f32[128,128]{1,0:T(8,128)}, u32[]{:S(2)}) copy-start(f32[128,128]{1,0:T(8,128)} %get-tuple-element.344) | copy-start | bytes 196612
  876.4 3.7 collective-permute-start
  881.2 7.7 collective-permute-start.1
  903.3 20.5 %collective-permute-start.2 = (bf16[6,24,128]{2,1,0:T(8,128)(2,1)S(1)}, bf16[6,24,128]{2,1,0:T(8,128)(2,1)S(1)}, u32[]{:S(2)}, u32[]{:S(2)}) collective-permute-start(bf16[6,24,128]{2,1,0:T(8,128)(2,1)S(1)} %get-tuple-element.318), channel_id=1, source_target_pairs={{0,16},{16,32},{32,48},{48,64},{64,80},{80,96},{96,112},{112,128},... | collective-permute-start | bytes 110600 | tf_op jit(solution)/shard_map/ppermute | solution.py:30
  907.5 16.4 %collective-permute-start.3 = (bf16[6,24,128]{2,1,0:T(8,128)(2,1)S(1)}, bf16[6,24,128]{2,1,0:T(8,128)(2,1)S(1)}, u32[]{:S(2)}, u32[]{:S(2)}) collective-permute-start(bf16[6,24,128]{2,1,0:T(8,128)(2,1)S(1)} %get-tuple-element.319), channel_id=1, source_target_pairs={{16,0},{32,16},{48,32},{64,48},{80,64},{96,80},{112,96},{128,112},... | collective-permute-start | bytes 110600 | tf_op jit(solution)/shard_map/ppermute | solution.py:32
  924.0 12.0 collective-permute-start.4
  927.9 8.1 collective-permute-start.5
  936.1 3.2 copy-start.13
  936.1 3.2 copy-start.14
  936.1 3.2 copy-start.15
  936.1 3.2 copy-start.16
  936.2 3.2 copy-start.17
  948.1 2.3 copy-start.18
  948.1 2.3 copy-start.20
  948.1 2.2 copy-start.21
  948.1 2.2 copy-start.23
  948.1 2.2 copy-start.24
  1028.0 35.8 %copy-start.1 = (bf16[24,24,128]{2,1,0:T(8,128)(2,1)}, bf16[24,24,128]{2,1,0:T(8,128)(2,1)S(1)}, u32[]{:S(2)}) copy-start(bf16[24,24,128]{2,1,0:T(8,128)(2,1)S(1)} %convert_element_type.310) | copy-start | bytes 442372
  1028.0 28.3 %collective-permute-start.6 = (bf16[24,24,128]{2,1,0:T(8,128)(2,1)S(1)}, bf16[24,24,128]{2,1,0:T(8,128)(2,1)S(1)}, u32[]{:S(2)}, u32[]{:S(2)}) collective-permute-start(bf16[24,24,128]{2,1,0:T(8,128)(2,1)S(1)} %convert_element_type.310), channel_id=1, source_target_pairs={{0,14},{2,0},{4,2},{6,4},{8,6},{10,8},{12,10},{14,12},{1,15},{3,1}... | collective-permute-start | bytes 442376 | tf_op jit(solution)/shard_map/ppermute | solution.py:20
  1056.3 7.4 collective-permute-start.7
  1275.2 34.0 %copy-start = (bf16[16,24,576]{2,1,0:T(8,128)(2,1)S(1)}, bf16[16,24,576]{2,1,0:T(8,128)(2,1)}, u32[]{:S(2)}) copy-start(bf16[16,24,576]{2,1,0:T(8,128)(2,1)} %param.26) | copy-start | bytes 1327108
